TPU v7x, 32 devices: a whole 2x2x4 slice. The times are simulated.
32 devices in a mesh: tm: 8 (over y, x, core), tile: 4 (over z).
Axes of the slice: x: 2, y: 2, z: 4, core: 2. Of those that a mesh axis runs over, the one named last changes fastest.
Arguments:
- movie: bfloat16 [32, 256, 1024], P('tm', 'tile'), may hold values from -6 to 6
- lift_weight: float32 [24], replicated, may hold values from -4 to 4
- lift_bias: float32 [24], replicated, may hold values from -3 to 3
- depth_kernel: float32 [3, 24, 9], replicated, may hold values from -2 to 2
- mix_weight: bfloat16 [3, 24, 24], replicated, may hold values from -1.25 to 1.25
- mix_bias: float32 [3, 24], replicated, may hold values from -3 to 3
- out_weight: float32 [24], replicated, may hold values from -1.25 to 1.25
- temporal_kernel: float32 [9], replicated, may hold values from -2 to 2
- footprints: bfloat16 [256, 256, 1024], P(None, 'tile', 'tm'), may hold values from -0.0625 to 0.0625
- slot_owner: int32 [8192, 1], P(('tm', 'tile')), may hold values from 0 to 31; in each aligned block of 256 rows (0 to 255, 256 to 511, ...) at most 16 rows name the same one
- slot_neuron: int32 [8192], P(('tm', 'tile')), may hold values from 0 to 319
Outputs:
- filtered: bfloat16 [32, 256, 1024], P(None, 'tile', 'tm')
- traces: float32 [10240, 32], P(('tm', 'tile'))
Inputs may be any that keep to these rules, and one draw needn't show every extreme that they name: `slot_owner`: within the rows of one device (256 aligned rows), no owner is named more than 16 times.
All inputs are finite; a program needn't handle non-finite values.
Results may differ from a plain program's by a relative error of at most 0.012.
Values may be sent and summed in bfloat16 or wider, within the bound.
A program may use at most 128 MiB of HBM per device.

v0:
```python
import jax
import jax.numpy as jnp
from jax import lax
from jax.experimental import pallas as pl
from jax.experimental.pallas import tpu as pltpu
from jax.sharding import PartitionSpec as P

LAYERS = 3
NEUR_DEV = 320
LANES = 128
ROWS_DOT = 4
PAD = 8


def split_halves(values):
    high = lax.reduce_precision(values, 8, 7)
    return high.astype(jnp.bfloat16), (values - high).astype(jnp.bfloat16)


def banded(taps, rows_out, rows_in, offset):
    out_row = jnp.arange(rows_out)[:, None, None]
    in_row = jnp.arange(rows_in)[None, :, None]
    hit = (in_row == out_row + offset + jnp.arange(3)[None, None, :]).astype(jnp.float32)
    extra = taps.ndim - 1
    hit = hit.reshape(hit.shape + (1,) * extra)
    return jnp.sum(hit * taps[None, None], axis=2)


def layer_weights(kernel, mixing):
    channels = mixing.shape[0]
    taps = kernel.reshape(channels, 3, 3).transpose(1, 2, 0)[:, :, :, None] * mixing.astype(
        jnp.float32
    )
    band = banded(taps, ROWS_DOT, ROWS_DOT + 2, 0)
    band = band.transpose(0, 4, 2, 1, 3)
    return band.reshape(ROWS_DOT * channels, 3 * (ROWS_DOT + 2) * channels).astype(jnp.bfloat16)


def first_weights(kernel, mixing, lift_weight, lift_bias):
    channels = mixing.shape[0]
    taps = kernel.reshape(channels, 3, 3).transpose(1, 2, 0)[:, :, :, None] * mixing.astype(
        jnp.float32
    )
    pieces = []
    for lift in (lift_weight, lift_bias):
        summed = jnp.sum(taps * lift[None, None, :, None], axis=2)
        band = banded(summed, 8, 16, 5).transpose(0, 3, 2, 1)
        pieces.extend(split_halves(band.reshape(8 * channels, 48)))
    return jnp.concatenate(pieces, axis=1)


def denoise_kernel(
    movie_ref,
    perm_ref,
    first_ref,
    second_ref,
    third_ref,
    lift_ref,
    bias_ref,
    out_ref,
    result_ref,
    frames_buf,
    inside_buf,
    feat1,
    feat2,
    den_buf,
):
    frames = movie_ref.shape[0]
    high = movie_ref.shape[1]
    width = movie_ref.shape[2]
    rows = high - 2 * PAD
    channels = lift_ref.shape[0]
    tiles = width // LANES
    chunk = 2 * LANES
    tile_index = lax.axis_index("tile")
    tile_count = lax.axis_size("tile")
    lane = lax.broadcasted_iota(jnp.int32, (1, LANES), 1)

    def store_edges(ref, where, low, top):
        ref[where, 0:LANES] = jnp.where(lane == 0, 0.0, pltpu.roll(top, 1, 1)).astype(ref.dtype)
        ref[where, (tiles + 1) * LANES : (tiles + 2) * LANES] = jnp.where(
            lane == LANES - 1, 0.0, pltpu.roll(low, LANES - 1, 1)
        ).astype(ref.dtype)

    flat = movie_ref[...].reshape(frames * high, width)
    permuted = jnp.dot(flat, perm_ref[...], preferred_element_type=jnp.float32)
    frames_buf[:, LANES : LANES + width] = permuted
    store_edges(
        frames_buf, slice(0, frames * high), permuted[:, :LANES], permuted[:, width - LANES :]
    )
    row = lax.broadcasted_iota(jnp.int32, (high, width + 2 * LANES), 0) - PAD
    col = lax.broadcasted_iota(jnp.int32, (high, width + 2 * LANES), 1)
    row = row + tile_index * rows
    keep = (row >= 0) & (row < rows * tile_count)
    keep = keep & (col != 0) & (col != width + 2 * LANES - 1)
    inside_buf[...] = jnp.where(keep, 1.0, 0.0)

    groups1 = (rows + 2 * (LAYERS - 1) + 7) // 8
    lift_w = lift_ref[:, 0:1]
    lift_b = lift_ref[:, 1:2]

    def first_group(frame, group):
        base = pl.multiple_of(frame * high + group * 8, 8)
        inner = pl.multiple_of(group * 8, 8)
        target = pl.multiple_of(group * (8 * channels), 16)
        bias = bias_ref[0]
        ends = {}
        for start in range(0, width, chunk):
            parts = [
                frames_buf[pl.ds(base, 16), start + j * LANES : start + j * LANES + chunk]
                for j in range(3)
            ]
            masks = [
                inside_buf[pl.ds(inner, 16), start + j * LANES : start + j * LANES + chunk]
                for j in range(3)
            ]
            window = parts[1]
            parts = [part.astype(jnp.bfloat16) for part in parts]
            masks = [mask.astype(jnp.bfloat16) for mask in masks]
            stack = jnp.concatenate(parts + parts + masks + masks, axis=0)
            mixed = jnp.dot(first_ref[...], stack, preferred_element_type=jnp.float32)
            lifted = jnp.concatenate(
                [lift_w * window[o + 6 : o + 7] + lift_b for o in range(8)], axis=0
            )
            value = lifted + jnp.maximum(mixed + bias, 0.0)
            feat1[pl.ds(target, 8 * channels), LANES + start : LANES + start + chunk] = (
                value.astype(jnp.bfloat16)
            )
            if start == 0:
                ends["low"] = value[:, :LANES]
            if start + chunk == width:
                ends["top"] = value[:, chunk - LANES :]
        store_edges(feat1, pl.ds(target, 8 * channels), ends["low"], ends["top"])

    def layer_rows(ref, weights_ref, bias, source, start):
        depth = (ROWS_DOT + 2) * channels
        parts = [
            ref[pl.ds(source, depth), start + j * LANES : start + j * LANES + chunk]
            for j in range(3)
        ]
        centre = parts[1].astype(jnp.float32)[channels : (ROWS_DOT + 1) * channels]
        stack = jnp.concatenate(parts, axis=0)
        mixed = jnp.dot(weights_ref[...], stack, preferred_element_type=jnp.float32)
        return centre + jnp.maximum(mixed + bias, 0.0)

    span = ROWS_DOT * channels

    def second_group(group):
        target = pl.multiple_of(group * span, 16)
        bias = bias_ref[1][:span]
        ends = {}
        for start in range(0, width, chunk):
            value = layer_rows(feat1, second_ref, bias, target, start)
            feat2[pl.ds(target, span), LANES + start : LANES + start + chunk] = value.astype(
                jnp.bfloat16
            )
            if start == 0:
                ends["low"] = value[:, :LANES]
            if start + chunk == width:
                ends["top"] = value[:, chunk - LANES :]
        store_edges(feat2, pl.ds(target, span), ends["low"], ends["top"])

    def third_group(frame, group):
        base = pl.multiple_of(frame * high + PAD + group * 8, 8)
        target = pl.multiple_of(frame * rows + group * 8, 8)
        bias = bias_ref[2][:span]
        out_weight = out_ref[:span]
        for start in range(0, width, chunk):
            sums = []
            for half in range(8 // ROWS_DOT):
                source = pl.multiple_of(group * (8 * channels) + half * span, 16)
                value = layer_rows(feat2, third_ref, bias, source, start) * out_weight
                sums.append(jnp.sum(value.reshape(ROWS_DOT, channels, chunk), axis=1))
            projected = jnp.concatenate(sums, axis=0) if len(sums) > 1 else sums[0]
            movie = frames_buf[pl.ds(base, 8), LANES + start : LANES + start + chunk]
            den_buf[pl.ds(target, 8), start : start + chunk] = movie + projected

    groups2 = -(-(rows + 2) // ROWS_DOT)
    zero_from = groups1 * 8 * channels
    if feat1.shape[0] > zero_from:
        feat1[zero_from:, :] = jnp.zeros((feat1.shape[0] - zero_from, feat1.shape[1]), jnp.bfloat16)

    def one_frame(frame, carry):
        def run1(group, inner):
            first_group(frame, group)
            return inner

        lax.fori_loop(0, groups1, run1, 0, unroll=3 if groups1 % 3 == 0 else 1)

        @pl.when(tile_index == 0)
        def _():
            feat1[0 : 2 * channels, :] = jnp.zeros((2 * channels, feat1.shape[1]), jnp.bfloat16)

        @pl.when(tile_index == tile_count - 1)
        def _():
            lower = (rows + 2) * channels
            feat1[lower : lower + 2 * channels, :] = jnp.zeros(
                (2 * channels, feat1.shape[1]), jnp.bfloat16
            )

        def run2(group, inner):
            second_group(group)
            return inner

        lax.fori_loop(0, groups2, run2, 0, unroll=4)

        def clear(lower, count):
            first = lower // 16 * 16
            size = -(-(lower + count) // 16) * 16 - first
            at = lax.broadcasted_iota(jnp.int32, (size, feat2.shape[1]), 0) + first
            old = feat2[first : first + size, :].astype(jnp.float32)
            outside = (at >= lower) & (at < lower + count)
            feat2[first : first + size, :] = jnp.where(outside, 0.0, old).astype(jnp.bfloat16)

        @pl.when(tile_index == 0)
        def _():
            clear(0, channels)

        @pl.when(tile_index == tile_count - 1)
        def _():
            clear((rows + 1) * channels, channels)

        def run3(group, inner):
            third_group(frame, group)
            return inner

        lax.fori_loop(0, rows // 8, run3, 0, unroll=2)
        return carry

    lax.fori_loop(0, frames, one_frame, 0)
    restored = lax.dot_general(
        den_buf[...].astype(jnp.bfloat16),
        perm_ref[...],
        (((1,), (1,)), ((), ())),
        preferred_element_type=jnp.float32,
    )
    result_ref[...] = restored.astype(jnp.bfloat16).reshape(frames, rows, width)


def denoise(movie, lift_weight, lift_bias, depth_kernel, mix_weight, mix_bias, out_weight):
    frames, rows, width = movie.shape
    channels = lift_weight.shape[0]
    count = lax.axis_size("tile")
    forward = [(i, i + 1) for i in range(count - 1)]
    backward = [(target, source) for source, target in forward]
    low = lax.ppermute(movie[:, rows - LAYERS :], "tile", forward)
    top = lax.ppermute(movie[:, :LAYERS], "tile", backward)
    blank = jnp.zeros((frames, PAD - LAYERS, width), movie.dtype)
    widened = jnp.concatenate([blank, low, movie, top, blank], axis=1)
    tiles = width // LANES
    place = jnp.arange(width)
    perm = (place[:, None] == (place % LANES * tiles + place // LANES)[None, :]).astype(
        jnp.bfloat16
    )
    first = first_weights(depth_kernel[0], mix_weight[0], lift_weight, lift_bias)
    second = layer_weights(depth_kernel[1], mix_weight[1])
    third = layer_weights(depth_kernel[2], mix_weight[2])
    lift = jnp.stack([lift_weight, lift_bias], axis=1)
    bias = jnp.tile(mix_bias, (1, 8))[:, :, None]
    out_col = jnp.tile(out_weight, 8)[:, None]
    groups1 = (rows + 2 * (LAYERS - 1) + 7) // 8
    groups2 = -(-(rows + 2) // ROWS_DOT)
    rows1 = max(groups1 * 8, groups2 * ROWS_DOT + 2)
    rows2 = groups2 * ROWS_DOT
    wide = width + 2 * LANES
    high = rows + 2 * PAD
    return pl.pallas_call(
        denoise_kernel,
        out_shape=jax.ShapeDtypeStruct(movie.shape, jnp.bfloat16),
        in_specs=[pl.BlockSpec(memory_space=pltpu.VMEM)] * 8,
        out_specs=pl.BlockSpec(memory_space=pltpu.VMEM),
        scratch_shapes=[
            pltpu.VMEM((frames * high, wide), jnp.float32),
            pltpu.VMEM((high, wide), jnp.float32),
            pltpu.VMEM((rows1 * channels, wide), jnp.bfloat16),
            pltpu.VMEM((rows2 * channels, wide), jnp.bfloat16),
            pltpu.VMEM((frames * rows, width), jnp.float32),
        ],
        compiler_params=pltpu.CompilerParams(vmem_limit_bytes=40 * 1024 * 1024),
    )(widened, perm, first, second, third, lift, bias, out_col)


def temporal(received, temporal_kernel):
    frame_count = received.shape[0]
    tap_count = temporal_kernel.shape[0]
    half_taps = tap_count // 2
    padded = jnp.pad(received.astype(jnp.float32), ((half_taps, half_taps), (0, 0), (0, 0)))
    summed = jnp.zeros(received.shape, jnp.float32)
    for tap_index in range(tap_count):
        summed = summed + temporal_kernel[tap_index] * padded[tap_index : tap_index + frame_count]
    return summed.astype(jnp.bfloat16)


def local(
    movie,
    lift_weight,
    lift_bias,
    depth_kernel,
    mix_weight,
    mix_bias,
    out_weight,
    temporal_kernel,
    footprints,
    slot_owner,
    slot_neuron,
):
    denoised = denoise(
        movie, lift_weight, lift_bias, depth_kernel, mix_weight, mix_bias, out_weight
    )
    filtered = temporal(
        lax.all_to_all(denoised, "tm", split_axis=2, concat_axis=0, tiled=True), temporal_kernel
    )
    frame_total, block_rows, block_cols = filtered.shape
    slot_total = footprints.shape[0]
    partial_value = lax.dot_general(
        footprints.reshape(slot_total, block_rows * block_cols),
        filtered.reshape(frame_total, block_rows * block_cols),
        (((1,), (1,)), ((), ())),
        preferred_element_type=jnp.float32,
    )
    tm_count = lax.axis_size("tm")
    tile_count = lax.axis_size("tile")
    device_count = tm_count * tile_count
    capacity = max(4, 2 * slot_total // device_count)
    target = slot_owner[:, 0]
    chosen = (target[:, None] == jnp.arange(device_count, dtype=jnp.int32)[None, :]).astype(
        jnp.int32
    )
    earlier = jnp.cumsum(chosen, axis=0) - chosen
    position = target * capacity + jnp.sum(earlier * chosen, axis=1)
    outgoing = (
        jnp.zeros((device_count * capacity, frame_total), jnp.float32)
        .at[position]
        .set(partial_value)
    )
    outgoing_ids = jnp.zeros((device_count * capacity,), jnp.int32).at[position].set(slot_neuron)
    arriving, arriving_ids = (
        lax.all_to_all(
            outgoing.reshape(device_count, capacity, frame_total).astype(jnp.bfloat16),
            ("tm", "tile"),
            split_axis=0,
            concat_axis=0,
            tiled=True,
        ).astype(jnp.float32),
        lax.all_to_all(
            outgoing_ids.reshape(device_count, capacity),
            ("tm", "tile"),
            split_axis=0,
            concat_axis=0,
            tiled=True,
        ),
    )
    arriving = arriving.reshape(device_count * capacity, frame_total)
    arriving_ids = arriving_ids.reshape(device_count * capacity)
    traces = jax.ops.segment_sum(arriving, arriving_ids, num_segments=NEUR_DEV)
    return (filtered, traces)


def solution(mesh):
    return jax.shard_map(
        local,
        mesh=mesh,
        in_specs=(
            P("tm", "tile", None),
            P(),
            P(),
            P(),
            P(),
            P(),
            P(),
            P(),
            P(None, "tile", "tm"),
            P(("tm", "tile"), None),
            P(("tm", "tile")),
        ),
        out_specs=(P(None, "tile", "tm"), P(("tm", "tile"), None)),
        check_vma=False,
    )
```

profile of v0, /device:TPU:0, one launch (start us, length us, event | category | flops | bytes accessed | tf_op | source)
XLA Modules:
  0.0 114.1 jit_solution(2879316095958703838)
XLA Ops:
  0.6 1.5 %fusion.48 = (bf16[4,3,1024]{2,1,0:T(4,128)(2,1)}, bf16[4,3,1024]{2,1,0:T(4,128)(2,1)}) fusion(bf16[4,64,1024]{2,1,0:T(8,128)(2,1)} %param.11), kind=kLoop, calls=%fused_computation.94 | loop fusion | bytes 98304 | tf_op jit(solution)/shard_map/slice | solution.py:247
  2.2 4.9 %collective-permute-start = (bf16[4,3,1024]{2,1,0:T(4,128)(2,1)}, bf16[4,3,1024]{2,1,0:T(4,128)(2,1)S(1)}, u32[]{:S(2)}, u32[]{:S(2)}) collective-permute-start(bf16[4,3,1024]{2,1,0:T(4,128)(2,1)} %get-tuple-element.20), channel_id=1, source_target_pairs={{0,1},{1,2},{2,3},{4,5},{5,6},{6,7},{8,9},{9,10},{10,11},{12,13},{... | collective-permute-start | bytes 73736 | tf_op jit(solution)/shard_map/ppermute | solution.py:246
  7.1 1.3 %collective-permute-start.1 = (bf16[4,3,1024]{2,1,0:T(4,128)(2,1)}, bf16[4,3,1024]{2,1,0:T(4,128)(2,1)S(1)}, u32[]{:S(2)}, u32[]{:S(2)}) collective-permute-start(bf16[4,3,1024]{2,1,0:T(4,128)(2,1)} %get-tuple-element.19), channel_id=1, source_target_pairs={{1,0},{2,1},{3,2},{5,4},{6,5},{7,6},{9,8},{10,9},{11,10},{13,12},{... | collective-permute-start | bytes 73736 | tf_op jit(solution)/shard_map/ppermute | solution.py:247
  8.4 0.7 bitcast_convert_fusion.1
  9.1 0.9 slice_reduce_fusion.1
  10.2 0.8 fusion.28
  12.1 0.9 fusion.2.perm_ref
  13.2 1.4 %multiply_reduce_fusion = (bf16[4,6,3,24,24]{4,3,2,1,0:T(8,128)(2,1)S(1)}, bf16[4,6,3,24,24]{4,3,2,1,0:T(8,128)(2,1)}) fusion(f32[3,3,24,24]{3,2,1,0:T(8,128)S(1)} %get-tuple-element.37, f32[4,6,3]{2,1,0:T(8,128)S(1)} %fusion.36, f32[3,3,24,24]{3,2,1,0:T(8,128)S(1)} %broadcast_multiply_fusion.1), kind=kLoop, calls=%fused_computation.7 | loop fusion | flops 414720 | bytes 207648 | tf_op jit(solution)/shard_map/reduce_sum | solution.py:26
  14.8 1.4 %copy.97 = bf16[4,24,3,6,24]{4,3,2,1,0:T(8,128)(2,1)S(1)} copy(bf16[4,24,3,6,24]{1,4,2,3,0:T(8,128)(2,1)} %bitcast.87) | data formatting | bytes 165888 | tf_op jit(solution)/shard_map/convert_element_type | solution.py:36
  16.1 0.9 reshape.202.second_ref
  17.4 1.0 reshape.203.third_ref
  18.4 0.9 tile.17.bias_ref
  20.1 2.0 %concatenate.6.movie_ref = bf16[4,80,1024]{2,1,0:T(8,128)(2,1)S(1)} concatenate(bf16[4,5,1024]{2,1,0:T(8,128)(2,1)S(1)} %broadcast_in_dim.8, bf16[4,3,1024]{2,1,0:T(4,128)(2,1)S(1)} %collective-permute-done, bf16[4,64,1024]{2,1,0:T(8,128)(2,1)} %param.11, bf16[4,3,1024]{2,1,0:T(4,128)(2,1)S(1)} %collective-permute-done.1, bf16[4,5,1024]{2,1,0:T(8,128)(2,1)S(1)} %broadcast_in_dim.8), dimensions={1} | concatenate | bytes 1310720 | tf_op jit(solution)/shard_map/concatenate | solution.py:249
  22.1 1.0 copy-done
  23.0 0.9 copy-done.1
  23.9 0.9 copy-done.2
  24.8 37.1 %shard_map.122 = bf16[4,64,1024]{2,1,0:T(8,128)(2,1)S(1)} custom-call(bf16[4,80,1024]{2,1,0:T(8,128)(2,1)S(1)} %concatenate.6.movie_ref, bf16[1024,1024]{1,0:T(8,128)(2,1)S(1)} %fusion.2.perm_ref, bf16[192,192]{1,0:T(8,128)(2,1)S(1)} %pad_maximum_fusion.first_ref, bf16[96,432]{1,0:T(8,128)(2,1)S(1)} %copy-done.1, bf16[96,432]{1,0:T(8,128)(2,1)S(1)} %copy-done.2, ...), custom_call_target="tpu_custom_call" | custom-call | tf_op jit(solution)/shard_map/pallas_call | solution.py:267
  62.7 1.5 %reshape.223 = bf16[8,2,16384]{2,1,0:T(2,128)(2,1)} reshape(bf16[1024,4,64]{2,1,0:T(4,128)(2,1)S(1)} %bitcast.85) | data formatting | bytes 1048576
  64.2 3.7 %all-to-all-start = ((bf16[8,2,16384]{2,1,0:T(2,128)(2,1)}), bf16[8,2,16384]{2,1,0:T(2,128)(2,1)S(1)}, u32[]{:S(2)}, u32[]{:S(2)}) async-start(bf16[8,2,16384]{2,1,0:T(2,128)(2,1)} %reshape.223), calls=%async_computation | async-start | bytes 1048576 | tf_op jit(solution)/shard_map/all_to_all | solution.py:311
  68.2 1.6 %scatter_custom_fusion = s32[512]{0:T(512)S(1)} fusion(s32[256]{0:T(256)S(1)} %bitcast.100, s32[256]{0:T(256)} %param.21, s32[]{:T(128)} %constant.43.clone.1), kind=kCustom, calls=%fused_computation.91 | custom fusion | bytes 2560 | tf_op jit(solution)/shard_map/scatter | solution.py:336
  71.2 6.5 %all-to-all-done = bf16[8,2,16384]{2,1,0:T(2,128)(2,1)S(1)} async-done(((bf16[8,2,16384]{2,1,0:T(2,128)(2,1)}), bf16[8,2,16384]{2,1,0:T(2,128)(2,1)S(1)}, u32[]{:S(2)}, u32[]{:S(2)}) %all-to-all-start) | async-done | bytes 524320 | tf_op jit(solution)/shard_map/all_to_all | solution.py:311
  77.7 5.2 %all-to-all-start.1 = ((s32[32,1,16]{2,1,0:T(1,128)}), s32[32,1,16]{2,1,0:T(1,128)S(1)}, u32[]{:S(2)}, u32[]{:S(2)}) async-start(s32[32,1,16]{2,1,0:T(1,128)} %bitcast.29), calls=%async_computation.1 | async-start | bytes 32768 | tf_op jit(solution)/shard_map/all_to_all | solution.py:345
  83.7 0.8 copy.90
  84.5 6.1 %fusion.15 = bf16[32,64,128]{2,1,0:T(8,128)(2,1)S(1)} fusion(f32[32,64,128]{2,1,0:T(8,128)S(1)} %bitcast.83, f32[]{:T(128)} %bitcast.23, f32[]{:T(128)} %bitcast.22, f32[]{:T(128)} %bitcast.21, f32[]{:T(128)} %bitcast.20, f32[]{:T(128)} %bitcast.19, f32[]{:T(128)} %bitcast.18, f32[]{:T(128)} %bitcast.17, f32[]{:T(128)} %bitcast.16, f32[]{:T(128)} %bitcast), kind=kLoop, calls=%fused_computation.28 | loop fusion | flops 4718592 | bytes 1572900 | tf_op jit(solution)/shard_map/convert_element_type | solution.py:291
  90.6 4.9 %fusion.3 = f32[256,32]{0,1:T(8,128)S(1)} fusion(bf16[256,64,128]{2,1,0:T(8,128)(2,1)} %param.19, bf16[32,64,128]{2,1,0:T(8,128)(2,1)S(1)} %fusion.15), kind=kOutput, calls=%fused_computation.18 | convolution fusion | flops 134217728 | bytes 4751360 | tf_op jit(solution)/shard_map/dot_general | solution.py:315
  95.6 1.2 %scatter_custom_fusion.1 = f32[512,32]{1,0:T(8,128)S(1)} fusion(s32[256]{0:T(256)S(1)} %bitcast.101, f32[256,32]{1,0:T(8,128)S(1)} %copy.95, f32[]{:T(128)} %constant.50.clone.1), kind=kCustom, calls=%fused_computation.45 | custom fusion | bytes 65540 | tf_op jit(solution)/shard_map/scatter | solution.py:334
  96.9 0.8 reshape.225
  97.6 5.7 %all-to-all-start.2 = ((bf16[32,2,256]{2,1,0:T(2,128)(2,1)}), bf16[32,2,256]{2,1,0:T(2,128)(2,1)S(1)}, u32[]{:S(2)}, u32[]{:S(2)}) async-start(bf16[32,2,256]{2,1,0:T(2,128)(2,1)} %reshape.225), calls=%async_computation.2 | async-start | bytes 65536 | tf_op jit(solution)/shard_map/all_to_all | solution.py:338
  103.9 0.7 reduce.11
  104.7 5.9 %all-to-all-done.2 = bf16[32,2,256]{2,1,0:T(2,128)(2,1)S(1)} async-done(((bf16[32,2,256]{2,1,0:T(2,128)(2,1)}), bf16[32,2,256]{2,1,0:T(2,128)(2,1)S(1)}, u32[]{:S(2)}, u32[]{:S(2)}) %all-to-all-start.2) | async-done | bytes 32800 | tf_op jit(solution)/shard_map/all_to_all | solution.py:338
  110.7 2.6 %scatter_custom_fusion.2 = f32[320,32]{1,0:T(8,128)S(1)} fusion(s32[512]{0:T(512)S(1)} %reshape.194, bf16[512,32]{1,0:T(8,128)(2,1)S(1)} %bitcast.91, f32[]{:T(128)} %constant.50.clone.1), kind=kCustom, calls=%fused_computation.41 | custom fusion | flops 32768 | bytes 172036 | tf_op jit(solution)/shard_map/scatter-add | solution.py:355
  113.3 0.7 copy.96
  (68 shorter events, 6.7 us)
Async XLA Ops:
  0.6 12.3 %copy-start.5 = (s32[256,1]{0,1:T(1,128)S(1)}, s32[256,1]{0,1:T(1,128)}, u32[]{:S(2)}) copy-start(s32[256,1]{0,1:T(1,128)} %param.20) | copy-start | bytes 3076
  2.2 17.9 %collective-permute-start = (bf16[4,3,1024]{2,1,0:T(4,128)(2,1)}, bf16[4,3,1024]{2,1,0:T(4,128)(2,1)S(1)}, u32[]{:S(2)}, u32[]{:S(2)}) collective-permute-start(bf16[4,3,1024]{2,1,0:T(4,128)(2,1)} %get-tuple-element.20), channel_id=1, source_target_pairs={{0,1},{1,2},{2,3},{4,5},{5,6},{6,7},{8,9},{9,10},{10,11},{12,13},{... | collective-permute-start | bytes 73736 | tf_op jit(solution)/shard_map/ppermute | solution.py:246
  7.1 12.9 %collective-permute-start.1 = (bf16[4,3,1024]{2,1,0:T(4,128)(2,1)}, bf16[4,3,1024]{2,1,0:T(4,128)(2,1)S(1)}, u32[]{:S(2)}, u32[]{:S(2)}) collective-permute-start(bf16[4,3,1024]{2,1,0:T(4,128)(2,1)} %get-tuple-element.19), channel_id=1, source_target_pairs={{1,0},{2,1},{3,2},{5,4},{6,5},{7,6},{9,8},{10,9},{11,10},{13,12},{... | collective-permute-start | bytes 73736 | tf_op jit(solution)/shard_map/ppermute | solution.py:247
  11.6 3.2 %copy-start.6 = (f32[24]{0:T(128)S(1)}, f32[24]{0:T(128)}, u32[]{:S(2)}) copy-start(f32[24]{0:T(128)} %param.12) | copy-start | bytes 292
  11.6 3.2 %copy-start.7 = (f32[24]{0:T(128)S(1)}, f32[24]{0:T(128)}, u32[]{:S(2)}) copy-start(f32[24]{0:T(128)} %param.13) | copy-start | bytes 292
  13.0 5.4 %copy-start.8 = (f32[3,24]{1,0:T(4,128)S(1)}, f32[3,24]{1,0:T(4,128)}, u32[]{:S(2)}) copy-start(f32[3,24]{1,0:T(4,128)} %param.16) | copy-start | bytes 868
  13.0 6.2 %copy-start.9 = (f32[24]{0:T(128)S(1)}, f32[24]{0:T(128)}, u32[]{:S(2)}) copy-start(f32[24]{0:T(128)} %param.17) | copy-start | bytes 292
  22.1 1.0 copy-start
  23.0 0.9 copy-start.1
  23.9 0.9 copy-start.2
  61.9 8.5 %copy-start.4 = (f32[9]{0:T(128)S(1)}, f32[9]{0:T(128)}, u32[]{:S(2)}) copy-start(f32[9]{0:T(128)} %param.18) | copy-start | bytes 112
  64.2 13.5 %all-to-all-start = ((bf16[8,2,16384]{2,1,0:T(2,128)(2,1)}), bf16[8,2,16384]{2,1,0:T(2,128)(2,1)S(1)}, u32[]{:S(2)}, u32[]{:S(2)}) async-start(bf16[8,2,16384]{2,1,0:T(2,128)(2,1)} %reshape.223), calls=%async_computation | async-start | bytes 1048576 | tf_op jit(solution)/shard_map/all_to_all | solution.py:311
  77.7 20.0 %all-to-all-start.1 = ((s32[32,1,16]{2,1,0:T(1,128)}), s32[32,1,16]{2,1,0:T(1,128)S(1)}, u32[]{:S(2)}, u32[]{:S(2)}) async-start(s32[32,1,16]{2,1,0:T(1,128)} %bitcast.29), calls=%async_computation.1 | async-start | bytes 32768 | tf_op jit(solution)/shard_map/all_to_all | solution.py:345
  90.6 6.3 %copy-start.3 = (bf16[32,64,128]{2,1,0:T(8,128)(2,1)}, bf16[32,64,128]{2,1,0:T(8,128)(2,1)S(1)}, u32[]{:S(2)}) copy-start(bf16[32,64,128]{2,1,0:T(8,128)(2,1)S(1)} %fusion.15) | copy-start | bytes 1572868
  97.6 13.0 %all-to-all-start.2 = ((bf16[32,2,256]{2,1,0:T(2,128)(2,1)}), bf16[32,2,256]{2,1,0:T(2,128)(2,1)S(1)}, u32[]{:S(2)}, u32[]{:S(2)}) async-start(bf16[32,2,256]{2,1,0:T(2,128)(2,1)} %reshape.225), calls=%async_computation.2 | async-start | bytes 65536 | tf_op jit(solution)/shard_map/all_to_all | solution.py:338
where the time goes:
time: 115 us; the launch traced here: 114 us
  Pallas kernels  37.1 us (32%)
  local copies, waits for them, and re-layouts  23 us (20%)
  starting transfers between devices  20.8 us (18%)
  other arithmetic  14.8 us (13%)
  waiting for transfers between devices  12.4 us (11%)
  matrix products  4.92 us (4%)
    pallas_call x1, Pallas kernels, denoise(): pl.pallas_call(denoise_kernel, out_shape=jax.ShapeDtypeStruct(movie.shape...  37.1 us
    unnamed x25, local copies, waits for them, and re-layouts  6.55 us
    all_to_all x1, waiting for transfers between devices, local(): lax.all_to_all(denoised, 'tm', split_axis=2, concat_axis=0, tiled=True)  6.49 us
    convert_element_type x1, other arithmetic, temporal(): return summed.astype(jnp.bfloat16)  6.09 us
    all_to_all x1, waiting for transfers between devices, local(): lax.all_to_all(outgoing.reshape(device_count, capacity, frame_total).asty...  5.88 us
    all_to_all x1, starting transfers between devices, local(): lax.all_to_all(outgoing.reshape(device_count, capacity, frame_total).asty...  5.66 us
    all_to_all x1, starting transfers between devices, local(): lax.all_to_all(outgoing_ids.reshape(device_count, capacity), ('tm', 'tile...  5.22 us
    dot_general x1, matrix products, local(): lax.dot_general(footprints.reshape(slot_total, block_rows * block_cols),...  4.92 us
  transfers between devices with their start and end apart: 5, of which 2 were waited for; matrix products, arithmetic and copies ran while one was open for 26% of the time, Pallas kernels for 0%

commit v1 on v0

--- a/solution.py
+++ b/solution.py
@@ -1,3 +1,5 @@
+import functools
+
 import jax
 import jax.numpy as jnp
 from jax import lax
@@ -12,64 +14,93 @@
 PAD = 8
 
 
-def split_halves(values):
-    high = lax.reduce_precision(values, 8, 7)
-    return high.astype(jnp.bfloat16), (values - high).astype(jnp.bfloat16)
-
-
-def banded(taps, rows_out, rows_in, offset):
-    out_row = jnp.arange(rows_out)[:, None, None]
-    in_row = jnp.arange(rows_in)[None, :, None]
-    hit = (in_row == out_row + offset + jnp.arange(3)[None, None, :]).astype(jnp.float32)
-    extra = taps.ndim - 1
-    hit = hit.reshape(hit.shape + (1,) * extra)
-    return jnp.sum(hit * taps[None, None], axis=2)
+EXACT = lax.Precision.HIGHEST
+
+
+def exact_dot(left, right, dims):
+    return lax.dot_general(
+        left, right, (dims, ((), ())), precision=EXACT, preferred_element_type=jnp.float32
+    )
+
+
+def one_hot(shape, hit):
+    first = lax.broadcasted_iota(jnp.int32, shape, 0)
+    second = lax.broadcasted_iota(jnp.int32, shape, 1)
+    return jnp.where(hit(first, second), 1.0, 0.0)
 
 
 def layer_weights(kernel, mixing):
     channels = mixing.shape[0]
-    taps = kernel.reshape(channels, 3, 3).transpose(1, 2, 0)[:, :, :, None] * mixing.astype(
-        jnp.float32
-    )
-    band = banded(taps, ROWS_DOT, ROWS_DOT + 2, 0)
-    band = band.transpose(0, 4, 2, 1, 3)
-    return band.reshape(ROWS_DOT * channels, 3 * (ROWS_DOT + 2) * channels).astype(jnp.bfloat16)
-
-
-def first_weights(kernel, mixing, lift_weight, lift_bias):
+    span = ROWS_DOT * channels
+    depth = (ROWS_DOT + 2) * channels
+    spread_rows = one_hot((span, channels), lambda r, d: r % channels == d)
+    spread_cols = one_hot((channels, 3 * depth), lambda c, s: s % channels == c)
+    by_row = lax.dot_general(
+        spread_rows.astype(jnp.bfloat16),
+        mixing,
+        (((1,), (1,)), ((), ())),
+        preferred_element_type=jnp.float32,
+    ).astype(jnp.bfloat16)
+    mixed = jnp.dot(by_row, spread_cols.astype(jnp.bfloat16), preferred_element_type=jnp.float32)
+    taps = exact_dot(kernel, spread_cols, ((0,), (0,)))
+    tap = lax.broadcasted_iota(jnp.int32, (9, 3 * depth), 0)
+    shift = lax.broadcasted_iota(jnp.int32, (9, 3 * depth), 1) // depth
+    out_row = lax.broadcasted_iota(jnp.int32, (span, 3 * depth), 0) // channels
+    in_row = lax.broadcasted_iota(jnp.int32, (span, 3 * depth), 1) % depth // channels
+    total = jnp.zeros((span, 3 * depth), jnp.float32)
+    for i in range(3):
+        chosen = jnp.sum(jnp.where(tap == 3 * i + shift, taps, 0.0), axis=0, keepdims=True)
+        total = total + jnp.where(in_row == out_row + i, chosen, 0.0)
+    return (total * mixed).astype(jnp.bfloat16)
+
+
+def first_weights(kernel, mixing, lift_pair):
     channels = mixing.shape[0]
-    taps = kernel.reshape(channels, 3, 3).transpose(1, 2, 0)[:, :, :, None] * mixing.astype(
-        jnp.float32
-    )
+    mixing = mixing.astype(jnp.float32)
+    spread_rows = one_hot((8 * channels, channels), lambda r, d: r % channels == d)
+    out_row = lax.broadcasted_iota(jnp.int32, (8 * channels, 48), 0) // channels
+    in_row = lax.broadcasted_iota(jnp.int32, (8 * channels, 48), 1) % 16
     pieces = []
-    for lift in (lift_weight, lift_bias):
-        summed = jnp.sum(taps * lift[None, None, :, None], axis=2)
-        band = banded(summed, 8, 16, 5).transpose(0, 3, 2, 1)
-        pieces.extend(split_halves(band.reshape(8 * channels, 48)))
-    return jnp.concatenate(pieces, axis=1)
+    for which in range(2):
+        gathered = exact_dot(mixing, kernel * lift_pair[:, which : which + 1], ((0,), (0,)))
+        gathered = exact_dot(spread_rows, gathered, ((1,), (0,)))
+        total = jnp.zeros((8 * channels, 48), jnp.float32)
+        for i in range(3):
+            pick = one_hot((9, 48), lambda tap, s: tap == 3 * i + s // 16)
+            term = exact_dot(gathered, pick, ((1,), (0,)))
+            total = total + jnp.where(in_row == out_row + 5 + i, term, 0.0)
+        high = total.astype(jnp.bfloat16)
+        pieces += [high, (total - high.astype(jnp.float32)).astype(jnp.bfloat16)]
+    return jnp.concatenate([piece.astype(jnp.float32) for piece in pieces], axis=1).astype(
+        jnp.bfloat16
+    )
 
 
 def denoise_kernel(
     movie_ref,
+    low_ref,
+    top_ref,
+    lift_weight_ref,
+    lift_bias_ref,
+    depth_ref,
+    mix_ref,
+    mix_bias_ref,
+    out_weight_ref,
+    result_ref,
     perm_ref,
     first_ref,
     second_ref,
     third_ref,
-    lift_ref,
-    bias_ref,
-    out_ref,
-    result_ref,
+    params_ref,
     frames_buf,
     inside_buf,
     feat1,
     feat2,
     den_buf,
 ):
-    frames = movie_ref.shape[0]
-    high = movie_ref.shape[1]
-    width = movie_ref.shape[2]
-    rows = high - 2 * PAD
-    channels = lift_ref.shape[0]
+    frames, rows, width = movie_ref.shape
+    high = rows + 2 * PAD
+    channels = lift_weight_ref.shape[1]
     tiles = width // LANES
     chunk = 2 * LANES
     tile_index = lax.axis_index("tile")
@@ -82,7 +113,37 @@
             lane == LANES - 1, 0.0, pltpu.roll(low, LANES - 1, 1)
         ).astype(ref.dtype)
 
-    flat = movie_ref[...].reshape(frames * high, width)
+    wide_place = lax.broadcasted_iota(jnp.int32, (1, width), 1)
+    source_col = wide_place % LANES * tiles + wide_place // LANES
+
+    def build(block, carry):
+        at = lax.broadcasted_iota(jnp.int32, (LANES, width), 0) + block * LANES
+        perm_ref[pl.ds(pl.multiple_of(block * LANES, LANES), LANES), :] = jnp.where(
+            at == source_col, 1.0, 0.0
+        ).astype(jnp.bfloat16)
+        return carry
+
+    lax.fori_loop(0, tiles, build, 0)
+    params = jnp.concatenate(
+        [lift_weight_ref[...], lift_bias_ref[...], out_weight_ref[...], mix_bias_ref[...]], axis=0
+    )
+    spread_rows = one_hot((8 * channels, channels), lambda r, d: r % channels == d)
+    params_ref[...] = exact_dot(spread_rows, params, ((1,), (1,)))
+    lift_pair = params_ref[:channels, 0:2]
+    first_ref[...] = first_weights(depth_ref[0], mix_ref[0], lift_pair)
+    second_ref[...] = layer_weights(depth_ref[1], mix_ref[1])
+    third_ref[...] = layer_weights(depth_ref[2], mix_ref[2])
+    pieces = []
+    for frame in range(frames):
+        blank = jnp.zeros((PAD - LAYERS, width), jnp.float32)
+        low = low_ref[frame].astype(jnp.float32)
+        top = top_ref[frame].astype(jnp.float32)
+        pieces += [
+            jnp.concatenate([blank, low], axis=0),
+            movie_ref[frame].astype(jnp.float32),
+            jnp.concatenate([top, blank], axis=0),
+        ]
+    flat = jnp.concatenate(pieces, axis=0).astype(jnp.bfloat16)
     permuted = jnp.dot(flat, perm_ref[...], preferred_element_type=jnp.float32)
     frames_buf[:, LANES : LANES + width] = permuted
     store_edges(
@@ -96,14 +157,14 @@
     inside_buf[...] = jnp.where(keep, 1.0, 0.0)
 
     groups1 = (rows + 2 * (LAYERS - 1) + 7) // 8
-    lift_w = lift_ref[:, 0:1]
-    lift_b = lift_ref[:, 1:2]
+    lift_w = params_ref[:channels, 0:1]
+    lift_b = params_ref[:channels, 1:2]
 
     def first_group(frame, group):
         base = pl.multiple_of(frame * high + group * 8, 8)
         inner = pl.multiple_of(group * 8, 8)
         target = pl.multiple_of(group * (8 * channels), 16)
-        bias = bias_ref[0]
+        bias = params_ref[:, 3:4]
         ends = {}
         for start in range(0, width, chunk):
             parts = [
@@ -147,7 +208,7 @@
 
     def second_group(group):
         target = pl.multiple_of(group * span, 16)
-        bias = bias_ref[1][:span]
+        bias = params_ref[:span, 4:5]
         ends = {}
         for start in range(0, width, chunk):
             value = layer_rows(feat1, second_ref, bias, target, start)
@@ -163,8 +224,8 @@
     def third_group(frame, group):
         base = pl.multiple_of(frame * high + PAD + group * 8, 8)
         target = pl.multiple_of(frame * rows + group * 8, 8)
-        bias = bias_ref[2][:span]
-        out_weight = out_ref[:span]
+        bias = params_ref[:span, 5:6]
+        out_weight = params_ref[:span, 2:3]
         for start in range(0, width, chunk):
             sums = []
             for half in range(8 // ROWS_DOT):
@@ -245,19 +306,6 @@
     backward = [(target, source) for source, target in forward]
     low = lax.ppermute(movie[:, rows - LAYERS :], "tile", forward)
     top = lax.ppermute(movie[:, :LAYERS], "tile", backward)
-    blank = jnp.zeros((frames, PAD - LAYERS, width), movie.dtype)
-    widened = jnp.concatenate([blank, low, movie, top, blank], axis=1)
-    tiles = width // LANES
-    place = jnp.arange(width)
-    perm = (place[:, None] == (place % LANES * tiles + place // LANES)[None, :]).astype(
-        jnp.bfloat16
-    )
-    first = first_weights(depth_kernel[0], mix_weight[0], lift_weight, lift_bias)
-    second = layer_weights(depth_kernel[1], mix_weight[1])
-    third = layer_weights(depth_kernel[2], mix_weight[2])
-    lift = jnp.stack([lift_weight, lift_bias], axis=1)
-    bias = jnp.tile(mix_bias, (1, 8))[:, :, None]
-    out_col = jnp.tile(out_weight, 8)[:, None]
     groups1 = (rows + 2 * (LAYERS - 1) + 7) // 8
     groups2 = -(-(rows + 2) // ROWS_DOT)
     rows1 = max(groups1 * 8, groups2 * ROWS_DOT + 2)
@@ -267,9 +315,14 @@
     return pl.pallas_call(
         denoise_kernel,
         out_shape=jax.ShapeDtypeStruct(movie.shape, jnp.bfloat16),
-        in_specs=[pl.BlockSpec(memory_space=pltpu.VMEM)] * 8,
+        in_specs=[pl.BlockSpec(memory_space=pltpu.VMEM)] * 9,
         out_specs=pl.BlockSpec(memory_space=pltpu.VMEM),
         scratch_shapes=[
+            pltpu.VMEM((width, width), jnp.bfloat16),
+            pltpu.VMEM((8 * channels, 192), jnp.bfloat16),
+            pltpu.VMEM((ROWS_DOT * channels, 3 * (ROWS_DOT + 2) * channels), jnp.bfloat16),
+            pltpu.VMEM((ROWS_DOT * channels, 3 * (ROWS_DOT + 2) * channels), jnp.bfloat16),
+            pltpu.VMEM((8 * channels, 6), jnp.float32),
             pltpu.VMEM((frames * high, wide), jnp.float32),
             pltpu.VMEM((high, wide), jnp.float32),
             pltpu.VMEM((rows1 * channels, wide), jnp.bfloat16),
@@ -277,18 +330,216 @@
             pltpu.VMEM((frames * rows, width), jnp.float32),
         ],
         compiler_params=pltpu.CompilerParams(vmem_limit_bytes=40 * 1024 * 1024),
-    )(widened, perm, first, second, third, lift, bias, out_col)
-
-
-def temporal(received, temporal_kernel):
-    frame_count = received.shape[0]
-    tap_count = temporal_kernel.shape[0]
-    half_taps = tap_count // 2
-    padded = jnp.pad(received.astype(jnp.float32), ((half_taps, half_taps), (0, 0), (0, 0)))
-    summed = jnp.zeros(received.shape, jnp.float32)
-    for tap_index in range(tap_count):
-        summed = summed + temporal_kernel[tap_index] * padded[tap_index : tap_index + frame_count]
-    return summed.astype(jnp.bfloat16)
+    )(
+        movie,
+        low,
+        top,
+        lift_weight[None],
+        lift_bias[None],
+        depth_kernel,
+        mix_weight,
+        mix_bias,
+        out_weight[None],
+    )
+
+
+def trace_kernel(
+    slot_capacity,
+    denoised_ref,
+    taps_ref,
+    footprints_ref,
+    owner_ref,
+    neuron_ref,
+    filtered_ref,
+    traces_ref,
+    received,
+    padded,
+    filtered_rows,
+    filtered_flat,
+    feet,
+    feet_rows,
+    feet_flat,
+    outgoing,
+    arriving,
+    load_sem,
+    own_sems,
+    frame_send,
+    frame_recv,
+    trace_send,
+    trace_recv,
+):
+    me_tm = lax.axis_index("tm")
+    me_tile = lax.axis_index("tile")
+    tm_count = lax.axis_size("tm")
+    tile_count = lax.axis_size("tile")
+    count = tm_count * tile_count
+    me = me_tm * tile_count + me_tile
+    frames = denoised_ref.shape[0]
+    slots, rows, cols = feet.shape
+    total, _, _ = received.shape
+    half = taps_ref.shape[0] // 2
+
+    load = pltpu.make_async_copy(footprints_ref, feet, load_sem)
+    load.start()
+    barrier = pltpu.get_barrier_semaphore()
+
+    def greet(offset, carry):
+        other = lax.rem(me + offset, count)
+        pl.semaphore_signal(
+            barrier,
+            inc=1,
+            device_id=(other // tile_count, lax.rem(other, tile_count)),
+            device_id_type=pl.DeviceIdType.MESH,
+        )
+        return carry
+
+    lax.fori_loop(1, count, greet, 0)
+    pl.semaphore_wait(barrier, count - 1)
+
+    def frame_copy(offset):
+        other = lax.rem(me_tm + offset, tm_count)
+        return pltpu.make_async_remote_copy(
+            src_ref=denoised_ref.at[:, :, pl.ds(pl.multiple_of(other * cols, cols), cols)],
+            dst_ref=received.at[pl.ds(me_tm * frames, frames)],
+            send_sem=frame_send.at[offset],
+            recv_sem=frame_recv.at[offset],
+            device_id=(other, me_tile),
+            device_id_type=pl.DeviceIdType.MESH,
+        )
+
+    own = pltpu.make_async_copy(
+        denoised_ref.at[:, :, pl.ds(pl.multiple_of(me_tm * cols, cols), cols)],
+        received.at[pl.ds(me_tm * frames, frames)],
+        own_sems.at[0],
+    )
+    own.start()
+    for offset in range(1, tm_count):
+        frame_copy(offset).start()
+
+    load.wait()
+
+    def widen(block, carry):
+        at = pl.multiple_of(block * 8, 8)
+        feet_rows[pl.ds(pl.multiple_of(block * (8 * rows), 8 * rows), 8 * rows), :] = (
+            feet[pl.ds(at, 8)].astype(jnp.float32).reshape(8 * rows, cols)
+        )
+        return carry
+
+    lax.fori_loop(0, slots // 8, widen, 0, unroll=4)
+
+    def flatten(row, carry):
+        at = pl.multiple_of(row * cols, cols)
+        feet_flat[:, pl.ds(at, cols)] = feet_rows[pl.ds(row, slots, stride=rows), :].astype(
+            jnp.bfloat16
+        )
+        return carry
+
+    lax.fori_loop(0, rows, flatten, 0, unroll=4)
+
+    owner = owner_ref[...]
+    device = lax.broadcasted_iota(jnp.int32, (slots, count), 1)
+    chosen = jnp.where(owner == device, 1.0, 0.0)
+    earlier = jnp.dot(
+        one_hot((slots, slots), lambda s, other: other < s).astype(jnp.bfloat16),
+        chosen.astype(jnp.bfloat16),
+        preferred_element_type=jnp.float32,
+    )
+    rank = jnp.sum(earlier * chosen, axis=1, keepdims=True)
+    place = owner.astype(jnp.float32) * float(slot_capacity) + rank
+    spot = lax.broadcasted_iota(jnp.int32, (slots, count * slot_capacity), 1).astype(jnp.float32)
+    packing = jnp.where(place == spot, 1.0, 0.0).astype(jnp.bfloat16)
+    neuron = neuron_ref[...]
+    digits_high = (neuron // 16).astype(jnp.float32)
+    digits_low = (neuron % 16).astype(jnp.float32)
+
+    for edge in (0, half + total):
+        padded[edge : edge + half] = jnp.zeros((half, rows, cols), jnp.float32)
+    own.wait()
+    for offset in range(1, tm_count):
+        frame_copy(offset).wait()
+
+    def unpack(frame, carry):
+        padded[frame + half] = received[frame].astype(jnp.float32)
+        return carry
+
+    lax.fori_loop(0, total, unpack, 0, unroll=4)
+    taps = [taps_ref[tap] for tap in range(2 * half + 1)]
+
+    def filter_frame(frame, carry):
+        summed = taps[0] * padded[frame]
+        for tap in range(1, 2 * half + 1):
+            summed = summed + taps[tap] * padded[frame + tap]
+        rounded = summed.astype(jnp.bfloat16)
+        filtered_ref[frame] = rounded
+        filtered_rows[pl.ds(pl.multiple_of(frame * rows, rows), rows), :] = rounded.astype(
+            jnp.float32
+        )
+        return carry
+
+    lax.fori_loop(0, total, filter_frame, 0, unroll=2)
+
+    def flatten_frames(row, carry):
+        at = pl.multiple_of(row * cols, cols)
+        filtered_flat[:, pl.ds(at, cols)] = filtered_rows[
+            pl.ds(row, total, stride=rows), :
+        ].astype(jnp.bfloat16)
+        return carry
+
+    lax.fori_loop(0, rows, flatten_frames, 0, unroll=4)
+    partial_value = lax.dot_general(
+        feet_flat[...],
+        filtered_flat[...],
+        (((1,), (1,)), ((), ())),
+        preferred_element_type=jnp.float32,
+    )
+    lane = lax.broadcasted_iota(jnp.int32, (slots, LANES), 1)
+    wide = jnp.concatenate(
+        [partial_value, jnp.zeros((slots, LANES - total), jnp.float32)], axis=1
+    )
+    wide = jnp.where(lane == total, digits_high, jnp.where(lane == total + 1, digits_low, wide))
+    packed = lax.dot_general(
+        packing,
+        wide.astype(jnp.bfloat16),
+        (((0,), (0,)), ((), ())),
+        preferred_element_type=jnp.float32,
+    )
+    outgoing[...] = packed.astype(jnp.bfloat16).reshape(count, slot_capacity, LANES)
+
+    def trace_copy(offset):
+        other = lax.rem(me + offset, count)
+        return pltpu.make_async_remote_copy(
+            src_ref=outgoing.at[other],
+            dst_ref=arriving.at[me],
+            send_sem=trace_send.at[offset],
+            recv_sem=trace_recv.at[offset],
+            device_id=(other // tile_count, lax.rem(other, tile_count)),
+            device_id_type=pl.DeviceIdType.MESH,
+        )
+
+    def send(offset, carry):
+        trace_copy(offset).start()
+        return carry
+
+    lax.fori_loop(1, count, send, 0)
+    own_traces = pltpu.make_async_copy(outgoing.at[me], arriving.at[me], own_sems.at[1])
+    own_traces.start()
+    own_traces.wait()
+
+    def finish(offset, carry):
+        trace_copy(offset).wait()
+        return carry
+
+    lax.fori_loop(1, count, finish, 0)
+    gathered = arriving[...].reshape(count * slot_capacity, LANES)
+    digits = gathered.astype(jnp.float32)
+    index = digits[:, total : total + 1] * 16.0 + digits[:, total + 1 : total + 2]
+    neurons = traces_ref.shape[0]
+    wanted = lax.broadcasted_iota(jnp.int32, (count * slot_capacity, neurons), 1)
+    member = jnp.where(index == wanted.astype(jnp.float32), 1.0, 0.0).astype(jnp.bfloat16)
+    summed = lax.dot_general(
+        member, gathered, (((0,), (0,)), ((), ())), preferred_element_type=jnp.float32
+    )
+    traces_ref[...] = summed[:, :total]
 
 
 def local(
@@ -307,52 +558,49 @@
     denoised = denoise(
         movie, lift_weight, lift_bias, depth_kernel, mix_weight, mix_bias, out_weight
     )
-    filtered = temporal(
-        lax.all_to_all(denoised, "tm", split_axis=2, concat_axis=0, tiled=True), temporal_kernel
-    )
-    frame_total, block_rows, block_cols = filtered.shape
-    slot_total = footprints.shape[0]
-    partial_value = lax.dot_general(
-        footprints.reshape(slot_total, block_rows * block_cols),
-        filtered.reshape(frame_total, block_rows * block_cols),
-        (((1,), (1,)), ((), ())),
-        preferred_element_type=jnp.float32,
-    )
     tm_count = lax.axis_size("tm")
-    tile_count = lax.axis_size("tile")
-    device_count = tm_count * tile_count
-    capacity = max(4, 2 * slot_total // device_count)
-    target = slot_owner[:, 0]
-    chosen = (target[:, None] == jnp.arange(device_count, dtype=jnp.int32)[None, :]).astype(
-        jnp.int32
-    )
-    earlier = jnp.cumsum(chosen, axis=0) - chosen
-    position = target * capacity + jnp.sum(earlier * chosen, axis=1)
-    outgoing = (
-        jnp.zeros((device_count * capacity, frame_total), jnp.float32)
-        .at[position]
-        .set(partial_value)
-    )
-    outgoing_ids = jnp.zeros((device_count * capacity,), jnp.int32).at[position].set(slot_neuron)
-    arriving, arriving_ids = (
-        lax.all_to_all(
-            outgoing.reshape(device_count, capacity, frame_total).astype(jnp.bfloat16),
-            ("tm", "tile"),
-            split_axis=0,
-            concat_axis=0,
-            tiled=True,
-        ).astype(jnp.float32),
-        lax.all_to_all(
-            outgoing_ids.reshape(device_count, capacity),
-            ("tm", "tile"),
-            split_axis=0,
-            concat_axis=0,
-            tiled=True,
+    count = tm_count * lax.axis_size("tile")
+    frames, rows, _ = movie.shape
+    slots, _, cols = footprints.shape
+    total = frames * tm_count
+    slot_capacity = max(16, 2 * slots // count)
+    half = temporal_kernel.shape[0] // 2
+    vmem = pl.BlockSpec(memory_space=pltpu.VMEM)
+    filtered, traces = pl.pallas_call(
+        functools.partial(trace_kernel, slot_capacity),
+        out_shape=(
+            jax.ShapeDtypeStruct((total, rows, cols), jnp.bfloat16),
+            jax.ShapeDtypeStruct((NEUR_DEV, total), jnp.float32),
         ),
-    )
-    arriving = arriving.reshape(device_count * capacity, frame_total)
-    arriving_ids = arriving_ids.reshape(device_count * capacity)
-    traces = jax.ops.segment_sum(arriving, arriving_ids, num_segments=NEUR_DEV)
+        in_specs=[
+            vmem,
+            pl.BlockSpec(memory_space=pltpu.SMEM),
+            pl.BlockSpec(memory_space=pl.ANY),
+            vmem,
+            vmem,
+        ],
+        out_specs=(vmem, vmem),
+        scratch_shapes=[
+            pltpu.VMEM((total, rows, cols), jnp.bfloat16),
+            pltpu.VMEM((total + 2 * half, rows, cols), jnp.float32),
+            pltpu.VMEM((total * rows, cols), jnp.float32),
+            pltpu.VMEM((total, rows * cols), jnp.bfloat16),
+            pltpu.VMEM((slots, rows, cols), jnp.bfloat16),
+            pltpu.VMEM((slots * rows, cols), jnp.float32),
+            pltpu.VMEM((slots, rows * cols), jnp.bfloat16),
+            pltpu.VMEM((count, slot_capacity, LANES), jnp.bfloat16),
+            pltpu.VMEM((count, slot_capacity, LANES), jnp.bfloat16),
+            pltpu.SemaphoreType.DMA,
+            pltpu.SemaphoreType.DMA((2,)),
+            pltpu.SemaphoreType.DMA((tm_count,)),
+            pltpu.SemaphoreType.DMA((tm_count,)),
+            pltpu.SemaphoreType.DMA((count,)),
+            pltpu.SemaphoreType.DMA((count,)),
+        ],
+        compiler_params=pltpu.CompilerParams(
+            collective_id=0, has_side_effects=True, vmem_limit_bytes=44 * 1024 * 1024
+        ),
+    )(denoised, temporal_kernel, footprints, slot_owner, slot_neuron[:, None])
     return (filtered, traces)
 
 

time: 115 us -> 84.9 us (0.74)
  Pallas kernels: 37.1 us -> 64.7 us
  other arithmetic: 14.8 us -> 0 us
  starting transfers between devices: 20.8 us -> 6.85 us
  waiting for transfers between devices: 12.4 us -> 0.01 us
  local copies, waits for them, and re-layouts: 23 us -> 12.1 us
  matrix products: 4.92 us -> 0 us
    pallas_call x0 -> x1, Pallas kernels: none -> 25.1 us  [local(): pl.pallas_call(functools.partial(trace_kernel, slot_capacity), out_shape=...]
    all_to_all x3 -> x0, starting transfers between devices: 14.6 us -> none  [the longest x1 5.66 us: local(): lax.all_to_all(outgoing.reshape(device_count, capacity, frame_total).asty...]
    all_to_all x3 -> x0, waiting for transfers between devices: 12.4 us -> none  [the longest x1 6.49 us: local(): lax.all_to_all(denoised, 'tm', split_axis=2, concat_axis=0, tiled=True)]
    convert_element_type x10 -> x0, other arithmetic: 7.98 us -> none  [the longest x1 6.09 us: temporal(): return summed.astype(jnp.bfloat16)]
    dot_general x1 -> x0, matrix products: 4.92 us -> none  [local(): lax.dot_general(footprints.reshape(slot_total, block_rows * block_cols),...]
    convert_element_type x5 -> x0, local copies, waits for them, and re-layouts: 4.41 us -> none  [the longest x4 3.63 us: layer_weights(): band.reshape(ROWS_DOT * channels, 3 * (ROWS_DOT + 2) * channels)]
    unnamed x25 -> x19, local copies, waits for them, and re-layouts: 6.55 us -> 9.65 us
    scatter x2 -> x0, local copies, waits for them, and re-layouts: 2.77 us -> none  [the longest x1 1.55 us: local(): jnp.zeros((device_count * capacity,), jnp.int32).at[position]]
  transfers between devices with their start and end apart: 5 -> 2, of which waited for: 2 -> 0; matrix products, arithmetic and copies ran while one was open for 26% -> 3% of each run, Pallas kernels for 0% -> 0%
where the time goes in v1:
time: 84.9 us; the launch traced here: 84.4 us
  Pallas kernels  64.7 us (76%)
  local copies, waits for them, and re-layouts  12.1 us (14%)
  starting transfers between devices  6.85 us (8%)
    pallas_call x1, Pallas kernels, denoise(): pl.pallas_call(denoise_kernel, out_shape=jax.ShapeDtypeStruct(movie.shape...  39.6 us
    pallas_call x1, Pallas kernels, local(): pl.pallas_call(functools.partial(trace_kernel, slot_capacity), out_shape=...  25.1 us
    unnamed x19, local copies, waits for them, and re-layouts  9.65 us
    ppermute x1, starting transfers between devices, denoise(): low = lax.ppermute(movie[:, rows - LAYERS:], 'tile', forward)  5.56 us
  transfers between devices with their start and end apart: 2, of which 0 were waited for; matrix products, arithmetic and copies ran while one was open for 3% of the time, Pallas kernels for 0%

profile of v1, /device:TPU:0, one launch (start us, length us, event | category | flops | bytes accessed | tf_op | source)
XLA Modules:
  0.0 84.4 jit_solution(17685363450703320288)
XLA Ops:
  0.6 0.9 %fusion = (bf16[4,3,1024]{2,1,0:T(4,128)(2,1)S(1)}, bf16[4,3,1024]{2,1,0:T(4,128)(2,1)S(1)}) fusion(bf16[4,64,1024]{2,1,0:T(8,128)(2,1)} %movie_ref.1), kind=kLoop, calls=%fused_computation | loop fusion | bytes 98304 | tf_op jit(solution)/shard_map/slice | solution.py:308
  1.5 1.3 %collective-permute-start.1 = (bf16[4,3,1024]{2,1,0:T(4,128)(2,1)S(1)}, bf16[4,3,1024]{2,1,0:T(4,128)(2,1)S(1)}, u32[]{:S(2)}, u32[]{:S(2)}) collective-permute-start(bf16[4,3,1024]{2,1,0:T(4,128)(2,1)S(1)} %get-tuple-element.6), channel_id=1, source_target_pairs={{1,0},{2,1},{3,2},{5,4},{6,5},{7,6},{9,8},{10,9},{11,10},{13,12},{... | collective-permute-start | bytes 73736 | tf_op jit(solution)/shard_map/ppermute | solution.py:308
  2.8 5.6 %collective-permute-start = (bf16[4,3,1024]{2,1,0:T(4,128)(2,1)S(1)}, bf16[4,3,1024]{2,1,0:T(4,128)(2,1)S(1)}, u32[]{:S(2)}, u32[]{:S(2)}) collective-permute-start(bf16[4,3,1024]{2,1,0:T(4,128)(2,1)S(1)} %get-tuple-element.7), channel_id=1, source_target_pairs={{0,1},{1,2},{2,3},{4,5},{5,6},{6,7},{8,9},{9,10},{10,11},{12,13},{... | collective-permute-start | bytes 73736 | tf_op jit(solution)/shard_map/ppermute | solution.py:307
  8.4 0.8 copy.16.depth_ref
  9.2 0.8 copy.17.owner_ref
  10.0 0.8 copy.18.neuron_ref
  10.8 0.0 collective-permute-done.1.top_ref
  10.9 0.0 collective-permute-done.low_ref
  10.9 0.0 copy-start.1
  10.9 1.0 %copy-done.1 = bf16[4,64,1024]{2,1,0:T(8,128)(2,1)S(1)} copy-done((bf16[4,64,1024]{2,1,0:T(8,128)(2,1)S(1)}, bf16[4,64,1024]{2,1,0:T(8,128)(2,1)}, u32[]{:S(2)}) %copy-start.1) | copy-done | bytes 524312
  11.9 0.0 copy-start.2
  11.9 0.7 copy-done.2
  12.6 0.0 copy-start.3
  12.6 0.7 copy-done.3
  13.3 0.0 copy-start.4
  13.3 0.7 copy-done.4
  14.0 0.0 copy-start.5
  14.0 0.7 copy-done.5
  14.6 0.0 copy-start.6
  14.6 0.7 copy-done.6
  15.3 39.6 %shard_map.122.denoised_ref = bf16[4,64,1024]{2,1,0:T(8,128)(2,1)S(1)} custom-call(bf16[4,64,1024]{2,1,0:T(8,128)(2,1)S(1)} %copy-done.1, bf16[4,3,1024]{2,1,0:T(4,128)(2,1)S(1)} %collective-permute-done.low_ref, bf16[4,3,1024]{2,1,0:T(4,128)(2,1)S(1)} %collective-permute-done.1.top_ref, f32[1,24]{1,0:T(1,128)S(1)} %bitcast.4, f32[1,24]{1,0:T(1,128)S(1)} %bitcast.5, ...), custom_call_target="tpu_custom_call" | custom-call | tf_op jit(solution)/shard_map/pallas_call | solution.py:315
  54.9 0.0 copy-start
  54.9 2.2 %copy-done = bf16[256,64,128]{2,1,0:T(8,128)(2,1)S(1)} copy-done((bf16[256,64,128]{2,1,0:T(8,128)(2,1)S(1)}, bf16[256,64,128]{2,1,0:T(8,128)(2,1)}, u32[]{:S(2)}) %copy-start) | copy-done | bytes 4194328
  57.1 0.0 copy-start.7
  57.1 0.7 copy-done.7
  57.8 25.1 %shard_map.123 = (bf16[32,64,128]{2,1,0:T(8,128)(2,1)S(1)}, f32[320,32]{1,0:T(8,128)S(1)}) custom-call(bf16[4,64,1024]{2,1,0:T(8,128)(2,1)S(1)} %shard_map.122.denoised_ref, f32[9]{0:T(128)S(1)} %copy-done.7, bf16[256,64,128]{2,1,0:T(8,128)(2,1)S(1)} %copy-done, s32[256,1]{1,0:T(8,128)S(1)} %copy.17.owner_ref, s32[256,1]{1,0:T(8,128)S(1)} %copy.18.neuron_ref), custom_call_target="tpu_custom_call" | custom-call | tf_op jit(solution)/shard_map/pallas_call | solution.py:569
  82.8 0.7 copy.19
  83.6 0.8 copy.21
Async XLA Ops:
  1.5 9.3 %collective-permute-start.1 = (bf16[4,3,1024]{2,1,0:T(4,128)(2,1)S(1)}, bf16[4,3,1024]{2,1,0:T(4,128)(2,1)S(1)}, u32[]{:S(2)}, u32[]{:S(2)}) collective-permute-start(bf16[4,3,1024]{2,1,0:T(4,128)(2,1)S(1)} %get-tuple-element.6), channel_id=1, source_target_pairs={{1,0},{2,1},{3,2},{5,4},{6,5},{7,6},{9,8},{10,9},{11,10},{13,12},{... | collective-permute-start | bytes 73736 | tf_op jit(solution)/shard_map/ppermute | solution.py:308
  2.8 8.0 %collective-permute-start = (bf16[4,3,1024]{2,1,0:T(4,128)(2,1)S(1)}, bf16[4,3,1024]{2,1,0:T(4,128)(2,1)S(1)}, u32[]{:S(2)}, u32[]{:S(2)}) collective-permute-start(bf16[4,3,1024]{2,1,0:T(4,128)(2,1)S(1)} %get-tuple-element.7), channel_id=1, source_target_pairs={{0,1},{1,2},{2,3},{4,5},{5,6},{6,7},{8,9},{9,10},{10,11},{12,13},{... | collective-permute-start | bytes 73736 | tf_op jit(solution)/shard_map/ppermute | solution.py:307
  10.9 1.0 %copy-start.1 = (bf16[4,64,1024]{2,1,0:T(8,128)(2,1)S(1)}, bf16[4,64,1024]{2,1,0:T(8,128)(2,1)}, u32[]{:S(2)}) copy-start(bf16[4,64,1024]{2,1,0:T(8,128)(2,1)} %movie_ref.1) | copy-start | bytes 1572868
  11.9 0.7 copy-start.2
  12.6 0.7 copy-start.3
  13.3 0.7 copy-start.4
  14.0 0.7 copy-start.5
  14.6 0.7 copy-start.6
  54.9 2.2 %copy-start = (bf16[256,64,128]{2,1,0:T(8,128)(2,1)S(1)}, bf16[256,64,128]{2,1,0:T(8,128)(2,1)}, u32[]{:S(2)}) copy-start(bf16[256,64,128]{2,1,0:T(8,128)(2,1)} %footprints_ref.1) | copy-start | bytes 12582916
  57.1 0.7 copy-start.7

commit v2 on v1

--- a/solution.py
+++ b/solution.py
@@ -10,7 +10,8 @@
 LAYERS = 3
 NEUR_DEV = 320
 LANES = 128
-ROWS_DOT = 4
+ROWS_DOT = 8
+HALO = 16
 PAD = 8
 
 
@@ -42,7 +43,7 @@
         preferred_element_type=jnp.float32,
     ).astype(jnp.bfloat16)
     mixed = jnp.dot(by_row, spread_cols.astype(jnp.bfloat16), preferred_element_type=jnp.float32)
-    taps = exact_dot(kernel, spread_cols, ((0,), (0,)))
+    taps = exact_dot(kernel, spread_cols, ((1,), (0,)))
     tap = lax.broadcasted_iota(jnp.int32, (9, 3 * depth), 0)
     shift = lax.broadcasted_iota(jnp.int32, (9, 3 * depth), 1) // depth
     out_row = lax.broadcasted_iota(jnp.int32, (span, 3 * depth), 0) // channels
@@ -62,7 +63,7 @@
     in_row = lax.broadcasted_iota(jnp.int32, (8 * channels, 48), 1) % 16
     pieces = []
     for which in range(2):
-        gathered = exact_dot(mixing, kernel * lift_pair[:, which : which + 1], ((0,), (0,)))
+        gathered = exact_dot(mixing, kernel * lift_pair[which : which + 1], ((0,), (1,)))
         gathered = exact_dot(spread_rows, gathered, ((1,), (0,)))
         total = jnp.zeros((8 * channels, 48), jnp.float32)
         for i in range(3):
@@ -80,12 +81,8 @@
     movie_ref,
     low_ref,
     top_ref,
-    lift_weight_ref,
-    lift_bias_ref,
-    depth_ref,
+    vectors_ref,
     mix_ref,
-    mix_bias_ref,
-    out_weight_ref,
     result_ref,
     perm_ref,
     first_ref,
@@ -100,7 +97,7 @@
 ):
     frames, rows, width = movie_ref.shape
     high = rows + 2 * PAD
-    channels = lift_weight_ref.shape[1]
+    channels = vectors_ref.shape[1]
     tiles = width // LANES
     chunk = 2 * LANES
     tile_index = lax.axis_index("tile")
@@ -124,20 +121,19 @@
         return carry
 
     lax.fori_loop(0, tiles, build, 0)
-    params = jnp.concatenate(
-        [lift_weight_ref[...], lift_bias_ref[...], out_weight_ref[...], mix_bias_ref[...]], axis=0
-    )
+    params = vectors_ref[0:8]
     spread_rows = one_hot((8 * channels, channels), lambda r, d: r % channels == d)
     params_ref[...] = exact_dot(spread_rows, params, ((1,), (1,)))
-    lift_pair = params_ref[:channels, 0:2]
-    first_ref[...] = first_weights(depth_ref[0], mix_ref[0], lift_pair)
-    second_ref[...] = layer_weights(depth_ref[1], mix_ref[1])
-    third_ref[...] = layer_weights(depth_ref[2], mix_ref[2])
+    first_ref[...] = first_weights(vectors_ref[8:17], mix_ref[0], params)
+    second_ref[...] = layer_weights(vectors_ref[24:33], mix_ref[1])
+    third_ref[...] = layer_weights(vectors_ref[40:49], mix_ref[2])
+    has_low = jnp.where(tile_index > 0, 1.0, 0.0)
+    has_top = jnp.where(tile_index < tile_count - 1, 1.0, 0.0)
     pieces = []
     for frame in range(frames):
         blank = jnp.zeros((PAD - LAYERS, width), jnp.float32)
-        low = low_ref[frame].astype(jnp.float32)
-        top = top_ref[frame].astype(jnp.float32)
+        low = low_ref[frame].astype(jnp.float32)[HALO - LAYERS :] * has_low
+        top = top_ref[frame].astype(jnp.float32)[:LAYERS] * has_top
         pieces += [
             jnp.concatenate([blank, low], axis=0),
             movie_ref[frame].astype(jnp.float32),
@@ -263,7 +259,7 @@
             second_group(group)
             return inner
 
-        lax.fori_loop(0, groups2, run2, 0, unroll=4)
+        lax.fori_loop(0, groups2, run2, 0, unroll=3 if groups2 % 3 == 0 else 1)
 
         def clear(lower, count):
             first = lower // 16 * 16
@@ -298,14 +294,75 @@
     result_ref[...] = restored.astype(jnp.bfloat16).reshape(frames, rows, width)
 
 
+def halo_kernel(movie_ref, low_ref, top_ref, from_low, from_top, send_sem, recv_sem):
+    me_tm = lax.axis_index("tm")
+    me = lax.axis_index("tile")
+    count = lax.axis_size("tile")
+    rows = movie_ref.shape[1]
+    above = lax.rem(me + count - 1, count)
+    below = lax.rem(me + 1, count)
+    barrier = pltpu.get_barrier_semaphore()
+    for other in (above, below):
+        pl.semaphore_signal(
+            barrier, inc=1, device_id=(me_tm, other), device_id_type=pl.DeviceIdType.MESH
+        )
+    pl.semaphore_wait(barrier, 2)
+    down = pltpu.make_async_remote_copy(
+        src_ref=movie_ref.at[:, rows - HALO :],
+        dst_ref=from_low,
+        send_sem=send_sem.at[0],
+        recv_sem=recv_sem.at[0],
+        device_id=(me_tm, below),
+        device_id_type=pl.DeviceIdType.MESH,
+    )
+    up = pltpu.make_async_remote_copy(
+        src_ref=movie_ref.at[:, :HALO],
+        dst_ref=from_top,
+        send_sem=send_sem.at[1],
+        recv_sem=recv_sem.at[1],
+        device_id=(me_tm, above),
+        device_id_type=pl.DeviceIdType.MESH,
+    )
+    down.start()
+    up.start()
+    down.wait()
+    up.wait()
+    low_ref[...] = from_low[...]
+    top_ref[...] = from_top[...]
+
+
 def denoise(movie, lift_weight, lift_bias, depth_kernel, mix_weight, mix_bias, out_weight):
     frames, rows, width = movie.shape
     channels = lift_weight.shape[0]
-    count = lax.axis_size("tile")
-    forward = [(i, i + 1) for i in range(count - 1)]
-    backward = [(target, source) for source, target in forward]
-    low = lax.ppermute(movie[:, rows - LAYERS :], "tile", forward)
-    top = lax.ppermute(movie[:, :LAYERS], "tile", backward)
+    vmem = pl.BlockSpec(memory_space=pltpu.VMEM)
+    band = jax.ShapeDtypeStruct((frames, HALO, width), movie.dtype)
+    low, top = pl.pallas_call(
+        halo_kernel,
+        out_shape=(band, band),
+        in_specs=[vmem],
+        out_specs=(vmem, vmem),
+        scratch_shapes=[
+            pltpu.VMEM(band.shape, band.dtype),
+            pltpu.VMEM(band.shape, band.dtype),
+            pltpu.SemaphoreType.DMA((2,)),
+            pltpu.SemaphoreType.DMA((2,)),
+        ],
+        compiler_params=pltpu.CompilerParams(collective_id=1, has_side_effects=True),
+    )(movie)
+    blank = jnp.zeros((2, channels), jnp.float32)
+    gap = jnp.zeros((LAYERS, 7, channels), jnp.float32)
+    taps = jnp.concatenate([depth_kernel.transpose(0, 2, 1), gap], axis=1)
+    vectors = jnp.concatenate(
+        [
+            lift_weight[None],
+            lift_bias[None],
+            out_weight[None],
+            mix_bias,
+            blank,
+            taps.reshape(LAYERS * 16, channels),
+        ],
+        axis=0,
+    )
     groups1 = (rows + 2 * (LAYERS - 1) + 7) // 8
     groups2 = -(-(rows + 2) // ROWS_DOT)
     rows1 = max(groups1 * 8, groups2 * ROWS_DOT + 2)
@@ -315,14 +372,14 @@
     return pl.pallas_call(
         denoise_kernel,
         out_shape=jax.ShapeDtypeStruct(movie.shape, jnp.bfloat16),
-        in_specs=[pl.BlockSpec(memory_space=pltpu.VMEM)] * 9,
+        in_specs=[vmem] * 5,
         out_specs=pl.BlockSpec(memory_space=pltpu.VMEM),
         scratch_shapes=[
             pltpu.VMEM((width, width), jnp.bfloat16),
             pltpu.VMEM((8 * channels, 192), jnp.bfloat16),
             pltpu.VMEM((ROWS_DOT * channels, 3 * (ROWS_DOT + 2) * channels), jnp.bfloat16),
             pltpu.VMEM((ROWS_DOT * channels, 3 * (ROWS_DOT + 2) * channels), jnp.bfloat16),
-            pltpu.VMEM((8 * channels, 6), jnp.float32),
+            pltpu.VMEM((8 * channels, 8), jnp.float32),
             pltpu.VMEM((frames * high, wide), jnp.float32),
             pltpu.VMEM((high, wide), jnp.float32),
             pltpu.VMEM((rows1 * channels, wide), jnp.bfloat16),
@@ -334,12 +391,8 @@
         movie,
         low,
         top,
-        lift_weight[None],
-        lift_bias[None],
-        depth_kernel,
+        vectors,
         mix_weight,
-        mix_bias,
-        out_weight[None],
     )
 
 
@@ -348,8 +401,7 @@
     denoised_ref,
     taps_ref,
     footprints_ref,
-    owner_ref,
-    neuron_ref,
+    slots_ref,
     filtered_ref,
     traces_ref,
     received,
@@ -436,7 +488,7 @@
 
     lax.fori_loop(0, rows, flatten, 0, unroll=4)
 
-    owner = owner_ref[...]
+    owner = slots_ref[:, 0:1]
     device = lax.broadcasted_iota(jnp.int32, (slots, count), 1)
     chosen = jnp.where(owner == device, 1.0, 0.0)
     earlier = jnp.dot(
@@ -448,7 +500,7 @@
     place = owner.astype(jnp.float32) * float(slot_capacity) + rank
     spot = lax.broadcasted_iota(jnp.int32, (slots, count * slot_capacity), 1).astype(jnp.float32)
     packing = jnp.where(place == spot, 1.0, 0.0).astype(jnp.bfloat16)
-    neuron = neuron_ref[...]
+    neuron = slots_ref[:, 1:2]
     digits_high = (neuron // 16).astype(jnp.float32)
     digits_low = (neuron % 16).astype(jnp.float32)
 
@@ -576,7 +628,6 @@
             vmem,
             pl.BlockSpec(memory_space=pltpu.SMEM),
             pl.BlockSpec(memory_space=pl.ANY),
-            vmem,
             vmem,
         ],
         out_specs=(vmem, vmem),
@@ -600,7 +651,12 @@
         compiler_params=pltpu.CompilerParams(
             collective_id=0, has_side_effects=True, vmem_limit_bytes=44 * 1024 * 1024
         ),
-    )(denoised, temporal_kernel, footprints, slot_owner, slot_neuron[:, None])
+    )(
+        denoised,
+        temporal_kernel,
+        footprints,
+        jnp.concatenate([slot_owner, slot_neuron[:, None]], axis=1),
+    )
     return (filtered, traces)
 
 

time: 84.9 us -> 91.1 us (1.073)
  Pallas kernels: 64.7 us -> 79.7 us
  starting transfers between devices: 6.85 us -> 0 us
  local copies, waits for them, and re-layouts: 12.1 us -> 9.54 us
    pallas_call x0 -> x1, Pallas kernels: none -> 12.4 us  [denoise(): pl.pallas_call(halo_kernel, out_shape=(band, band), in_specs=[vmem], out_...]
    ppermute x2 -> x0, starting transfers between devices: 6.85 us -> none  [the longest x1 5.56 us: denoise(): low = lax.ppermute(movie[:, rows - LAYERS:], 'tile', forward)]
    pallas_call x1, Pallas kernels: 39.6 us -> 41.9 us  [denoise(): pl.pallas_call(denoise_kernel, out_shape=jax.ShapeDtypeStruct(movie.shape...]
    unnamed x19 -> x14, local copies, waits for them, and re-layouts: 9.65 us -> 7.92 us
  transfers between devices with their start and end apart: 2 -> 0, of which waited for: 0 -> 0; matrix products, arithmetic and copies ran while one was open for 3% -> 0% of each run, Pallas kernels for 0% -> 0%
where the time goes in v2:
time: 91.1 us; the launch traced here: 90.6 us
  Pallas kernels  79.7 us (87%)
  local copies, waits for them, and re-layouts  9.54 us (10%)
    pallas_call x1, Pallas kernels, denoise(): pl.pallas_call(denoise_kernel, out_shape=jax.ShapeDtypeStruct(movie.shape...  41.9 us
    pallas_call x1, Pallas kernels, local(): pl.pallas_call(functools.partial(trace_kernel, slot_capacity), out_shape=...  25.4 us
    pallas_call x1, Pallas kernels, denoise(): pl.pallas_call(halo_kernel, out_shape=(band, band), in_specs=[vmem], out_...  12.4 us
    unnamed x14, local copies, waits for them, and re-layouts  7.92 us

profile of v2, /device:TPU:0, one launch (start us, length us, event | category | flops | bytes accessed | tf_op | source)
XLA Modules:
  0.0 90.6 jit_solution(9761196598612043974)
XLA Ops:
  0.6 0.7 pad_add_fusion
  1.3 0.7 copy.40
  2.1 0.8 concatenate.10.vectors_ref
  2.8 0.1 copy.38.slots_ref
  3.0 12.4 %shard_map.122 = (bf16[4,16,1024]{2,1,0:T(8,128)(2,1)}, bf16[4,16,1024]{2,1,0:T(8,128)(2,1)}) custom-call(bf16[4,64,1024]{2,1,0:T(8,128)(2,1)} %movie_ref.3), custom_call_target="tpu_custom_call" | custom-call | tf_op jit(solution)/shard_map/pallas_call | solution.py:339
  15.4 0.0 copy-start.1
  15.4 1.0 %copy-done.1 = bf16[4,64,1024]{2,1,0:T(8,128)(2,1)S(1)} copy-done((bf16[4,64,1024]{2,1,0:T(8,128)(2,1)S(1)}, bf16[4,64,1024]{2,1,0:T(8,128)(2,1)}, u32[]{:S(2)}) %copy-start.1) | copy-done | bytes 524312
  16.4 0.0 copy-start.2
  16.4 0.9 copy-done.2
  17.3 0.0 copy-start.3
  17.4 0.9 copy-done.3
  18.3 0.0 copy-start.4
  18.3 0.7 copy-done.4
  19.0 41.9 %shard_map.123.denoised_ref = bf16[4,64,1024]{2,1,0:T(8,128)(2,1)S(1)} custom-call(bf16[4,64,1024]{2,1,0:T(8,128)(2,1)S(1)} %copy-done.1, bf16[4,16,1024]{2,1,0:T(8,128)(2,1)S(1)} %copy-done.2, bf16[4,16,1024]{2,1,0:T(8,128)(2,1)S(1)} %copy-done.3, f32[56,24]{1,0:T(8,128)S(1)} %concatenate.10.vectors_ref, bf16[3,24,24]{2,1,0:T(8,128)(2,1)S(1)} %copy-done.4), custom_call_target="tpu_custom_call" | custom-call | tf_op jit(solution)/shard_map/pallas_call | solution.py:372
  60.9 0.0 copy-start
  60.9 2.2 %copy-done = bf16[256,64,128]{2,1,0:T(8,128)(2,1)S(1)} copy-done((bf16[256,64,128]{2,1,0:T(8,128)(2,1)S(1)}, bf16[256,64,128]{2,1,0:T(8,128)(2,1)}, u32[]{:S(2)}) %copy-start) | copy-done | bytes 4194328
  63.1 0.0 copy-start.5
  63.1 0.7 copy-done.5
  63.7 25.4 %shard_map.124 = (bf16[32,64,128]{2,1,0:T(8,128)(2,1)S(1)}, f32[320,32]{1,0:T(8,128)S(1)}) custom-call(bf16[4,64,1024]{2,1,0:T(8,128)(2,1)S(1)} %shard_map.123.denoised_ref, f32[9]{0:T(128)S(1)} %copy-done.5, bf16[256,64,128]{2,1,0:T(8,128)(2,1)S(1)} %copy-done, s32[256,2]{1,0:T(8,128)S(1)} %copy.38.slots_ref), custom_call_target="tpu_custom_call" | custom-call | tf_op jit(solution)/shard_map/pallas_call | solution.py:621
  89.1 0.7 copy.39
  89.8 0.8 copy.42
  (2 shorter events, 0.0 us)
Async XLA Ops:
  15.4 1.0 %copy-start.1 = (bf16[4,64,1024]{2,1,0:T(8,128)(2,1)S(1)}, bf16[4,64,1024]{2,1,0:T(8,128)(2,1)}, u32[]{:S(2)}) copy-start(bf16[4,64,1024]{2,1,0:T(8,128)(2,1)} %movie_ref.3) | copy-start | bytes 1572868
  16.4 0.9 copy-start.2
  17.3 0.9 copy-start.3
  18.3 0.7 copy-start.4
  60.9 2.2 %copy-start = (bf16[256,64,128]{2,1,0:T(8,128)(2,1)S(1)}, bf16[256,64,128]{2,1,0:T(8,128)(2,1)}, u32[]{:S(2)}) copy-start(bf16[256,64,128]{2,1,0:T(8,128)(2,1)} %footprints_ref.1) | copy-start | bytes 12582916
  63.1 0.7 copy-start.5
